TPU v7x, 32 devices: a whole 2x2x4 slice. The times are simulated.
32 devices in a mesh: dp: 16 (over z, y, core), blk: 2 (over x).
Axes of the slice: x: 2, y: 2, z: 4, core: 2. Of those that a mesh axis runs over, the one named last changes fastest.
Arguments:
- tokens: bfloat16 [48, 1024, 768], P('dp', 'blk'), may hold values from -6 to 6
- query_weight: bfloat16 [768, 768], replicated, may hold values from -0.21875 to 0.21875
- query_bias: bfloat16 [768], replicated, may hold values from -3 to 3
- key_weight: bfloat16 [768, 768], replicated, may hold values from -0.21875 to 0.21875
- value_weight: bfloat16 [768, 768], replicated, may hold values from -0.21875 to 0.21875
- value_bias: bfloat16 [768], replicated, may hold values from -3 to 3
- out_weight: bfloat16 [768, 768], replicated, may hold values from -1.75 to 1.75
- out_bias: bfloat16 [768], replicated, may hold values from -3 to 3
- gain_one: bfloat16 [768], replicated, may hold values from 0.099609375 to 1.8984375
- shift_one: bfloat16 [768], replicated, may hold values from -3 to 3
- up_weight: bfloat16 [768, 3072], replicated, may hold values from -0.21875 to 0.21875
- up_bias: bfloat16 [3072], replicated, may hold values from -3 to 3
- down_weight: bfloat16 [3072, 768], replicated, may hold values from -0.109375 to 0.109375
- down_bias: bfloat16 [768], replicated, may hold values from -3 to 3
- gain_two: bfloat16 [768], replicated, may hold values from 0.099609375 to 1.8984375
- shift_two: bfloat16 [768], replicated, may hold values from -3 to 3
- group_ids: int32 [48, 1024], P('dp', 'blk'), may hold values from 0 to 4, as said below
- valid_mask: int32 [48, 1024], P('dp', 'blk'), may hold values from 0 to 1, as said below
- cotangent: bfloat16 [48, 1024, 768], P('dp', 'blk'), may hold values from -6 to 6
Outputs:
- block_out: bfloat16 [48, 1024, 768], P('dp', 'blk')
- tokens_gradient: bfloat16 [48, 1024, 768], P('dp', 'blk')
- query_weight_gradient: float32 [768, 768], P(('dp', 'blk'))
- query_bias_gradient: float32 [768], P(('dp', 'blk'))
- key_weight_gradient: float32 [768, 768], P(('dp', 'blk'))
- value_weight_gradient: float32 [768, 768], P(('dp', 'blk'))
- value_bias_gradient: float32 [768], P(('dp', 'blk'))
- out_weight_gradient: float32 [768, 768], P(('dp', 'blk'))
- out_bias_gradient: float32 [768], P(('dp', 'blk'))
- gain_one_gradient: float32 [768], P(('dp', 'blk'))
- shift_one_gradient: float32 [768], P(('dp', 'blk'))
- up_weight_gradient: float32 [768, 3072], P(('dp', 'blk'))
- up_bias_gradient: float32 [3072], P(('dp', 'blk'))
- down_weight_gradient: float32 [3072, 768], P(('dp', 'blk'))
- down_bias_gradient: float32 [768], P(('dp', 'blk'))
- gain_two_gradient: float32 [768], P(('dp', 'blk'))
- shift_two_gradient: float32 [768], P(('dp', 'blk'))
Inputs may be any that keep to these rules, and one draw needn't show every extreme that they name: `group_ids`: group numbers never fall along a sequence and every group has a used slot. In each aligned block of 3 sequences one sequence, drawn from the seed, is group 0 in all its slots; the others have 5 groups. `valid_mask`: the unused slots of a group are its last ones.
All inputs are finite; a program needn't handle non-finite values.
Results may differ from a plain program's by a relative error of at most 0.02.
Values may be sent and summed in bfloat16 or wider, within the bound.
A program may use at most 320 MiB of HBM per device.

v0:
```python
import functools
import math

import jax
import jax.numpy as jnp
from jax import lax
from jax.experimental import pallas as pl
from jax.experimental.pallas import tpu as pltpu
from jax.sharding import PartitionSpec as P

HEAD = 64
PAIR = 2 * HEAD
EPSILON = 1e-12
MASKED = -1e30
FLOOR = -3e38
SCALE = HEAD**-0.5
EXPO = SCALE * math.log2(math.e)
NN = (((1,), (0,)), ((), ()))
NT = (((1,), (1,)), ((), ()))
F32 = jnp.float32
BF16 = jnp.bfloat16
MIB = 1 << 20
FEED_ROWS = 256


def dot(left, right, dims=NN):
    return lax.dot_general(left, right, dims, preferred_element_type=F32)


def whole_spec(shape):
    return pl.BlockSpec(shape, lambda *_: (0,) * len(shape), pipeline_mode=pl.Buffered(1))


def params(limit):
    return pltpu.CompilerParams(vmem_limit_bytes=limit * MIB)


def cost(flops, touched, exps=0):
    return pl.CostEstimate(flops=int(flops), bytes_accessed=int(touched), transcendentals=int(exps))


def project_kernel(has_query, *refs):
    if has_query:
        x_ref, bias_ref, wq_ref, wk_ref, wv_ref, q_ref, k_ref, v_ref = refs
    else:
        x_ref, bias_ref, wk_ref, wv_ref, k_ref, v_ref = refs
    x = x_ref[0]
    if has_query:
        q_ref[0] = ((dot(x, wq_ref[...]) + bias_ref[0:1]) * EXPO).astype(BF16)
    k_ref[0] = dot(x, wk_ref[...]).astype(BF16)
    v_ref[0] = (dot(x, wv_ref[...]) + bias_ref[1:2]).astype(BF16)


def project(x, bias, weights):
    seqs, length, features = x.shape
    tile = math.gcd(length, 512)
    grid = (seqs, length // tile)
    row_spec = pl.BlockSpec((1, tile, features), lambda s, i: (s, i, 0))
    return pl.pallas_call(
        functools.partial(project_kernel, len(weights) == 3),
        grid=grid,
        in_specs=[row_spec, whole_spec(bias.shape)] + [whole_spec(w.shape) for w in weights],
        out_specs=[row_spec] * len(weights),
        out_shape=[jax.ShapeDtypeStruct(x.shape, BF16)] * len(weights),
        compiler_params=params(60),
        cost_estimate=cost(
            2 * x.size * features * len(weights), 2 * x.size * (1 + len(weights))
        ),
        name="project",
    )(x, bias, *weights)


def low_lanes():
    return lax.broadcasted_iota(jnp.int32, (1, PAIR), 1) < HEAD


def attend_group(q, qm, sources, o_ref, lse_ref):
    length = q.shape[0]
    tile = math.gcd(length, 512)
    low = low_lanes()
    one = jnp.ones((1, PAIR), BF16)
    todo = [
        (pair, row, head)
        for pair in range(q.shape[1] // PAIR)
        for row in range(0, length, tile)
        for head in range(2)
    ]

    def lanes_of(pair):
        return slice(pair * PAIR, (pair + 1) * PAIR)

    def mine_of(head):
        return ~low if head else low

    def scores_of(pair, row, head):
        mine, lanes = mine_of(head), lanes_of(pair)
        q_side = jnp.where(mine, q[row : row + tile, lanes], qm[row : row + tile])
        return [dot(q_side, jnp.where(mine, k[:, lanes], km), NT) for k, km, _ in sources]

    ahead = scores_of(*todo[0])
    for i, (pair, row, head) in enumerate(todo):
        scores = ahead
        if i + 1 < len(todo):
            ahead = scores_of(*todo[i + 1])
        top = functools.reduce(
            jnp.maximum, [jnp.max(part, axis=-1, keepdims=True) for part in scores]
        )
        weights = [jnp.exp2(part - top).astype(BF16) for part in scores]
        total = sum(
            dot(w, jnp.where(mine_of(head), v[:, lanes_of(pair)], one))
            for w, (_, _, v) in zip(weights, sources)
        )
        if head == 0:
            earlier, earlier_top = total, top
            continue
        totals = pltpu.roll(jnp.where(low, total, earlier), HEAD, 1)
        rows = slice(row, row + tile)
        o_ref[rows, lanes_of(pair)] = (jnp.where(low, earlier, total) / totals).astype(BF16)
        lse = (jnp.where(low, earlier_top, top) + jnp.log2(totals)).T
        lse_ref[pair, 0:1, rows] = lse[0:1]
        lse_ref[pair, 1:2, rows] = lse[HEAD : HEAD + 1]


def attend_kernel(q_ref, qm_ref, ko_ref, kmo_ref, vo_ref, kr_ref, kmr_ref, vr_ref, o_ref, lse_ref):
    sources = [(ko_ref[0], kmo_ref[0], vo_ref[0]), (kr_ref[0], kmr_ref[0], vr_ref[0])]
    attend_group(q_ref[0], qm_ref[0], sources, o_ref.at[0], lse_ref.at[0])


def pair_spec(length, lanes):
    return pl.BlockSpec((1, length, lanes), lambda s, h: (s, 0, h))


def mask_spec(length):
    return pl.BlockSpec((1, length, PAIR), lambda s, h: (s, 0, 0))


def lse_spec(length, lanes):
    return pl.BlockSpec((1, lanes // PAIR, 8, length), lambda s, h: (s, h, 0, 0))


def attend(q, qm, own, rem):
    seqs, length, features = q.shape
    lanes = math.gcd(features, 2 * PAIR)
    other = rem[0].shape[1]
    own_spec, rem_spec = pair_spec(length, lanes), pair_spec(other, lanes)
    return pl.pallas_call(
        attend_kernel,
        grid=(seqs, features // lanes),
        in_specs=[own_spec, mask_spec(length)]
        + [own_spec, mask_spec(length), own_spec]
        + [rem_spec, mask_spec(other), rem_spec],
        out_specs=[own_spec, lse_spec(length, lanes)],
        out_shape=[
            jax.ShapeDtypeStruct(q.shape, BF16),
            jax.ShapeDtypeStruct((seqs, features // PAIR, 8, length), F32),
        ],
        compiler_params=params(60),
        cost_estimate=cost(
            16 * q.size * (length + other), 2 * q.size * 6, q.size * (length + other) // HEAD
        ),
        name="attend",
    )(q, qm, *own, *rem)


def attend_back_part(q, qm, g, lse_ref, k, km, v, dk_ref, dv_ref):
    low = low_lanes()
    none = jnp.zeros((1, PAIR), BF16)
    pairs = q.shape[1] // PAIR
    todo = [(pair, head) for pair in range(pairs) for head in range(2)]

    def lanes_of(pair):
        return slice(pair * PAIR, (pair + 1) * PAIR)

    def mine_of(head):
        return ~low if head else low

    def products(pair, head):
        mine, lanes = mine_of(head), lanes_of(pair)
        return (
            dot(jnp.where(mine, k[:, lanes], km), jnp.where(mine, q[:, lanes], qm), NT),
            dot(jnp.where(mine, v[:, lanes], none), g[:, lanes], NT),
        )

    found = []
    ahead = products(*todo[0])
    for i, (pair, head) in enumerate(todo):
        scores, grads = ahead
        if i + 1 < len(todo):
            ahead = products(*todo[i + 1])
        lanes, mine = lanes_of(pair), mine_of(head)
        if head == 0:
            k_t = k[:, lanes].T
            dk = dv = 0.0
            dq = []
        probs = jnp.exp2(scores - lse_ref[pair, head : head + 1, :])
        grads = (probs * (grads - lse_ref[pair, 2 + head : 3 + head, :])).astype(BF16)
        dv += dot(probs.astype(BF16), jnp.where(mine, g[:, lanes], none))
        dk += dot(grads, jnp.where(mine, q[:, lanes], none))
        dq.append(dot(k_t[head * HEAD : (head + 1) * HEAD], grads))
        if head == 1:
            dk_ref[:, lanes] = (dk * (SCALE / EXPO)).astype(BF16)
            dv_ref[:, lanes] = dv.astype(BF16)
            found.append(jnp.concatenate(dq, axis=0))
    return found


def attend_back_kernel(q_ref, qm_ref, g_ref, lse_ref, ko_ref, kmo_ref, vo_ref, kr_ref, kmr_ref,
                       vr_ref, dq_ref, dko_ref, dvo_ref, dkr_ref, dvr_ref):
    parts = ((ko_ref, kmo_ref, vo_ref, dko_ref, dvo_ref), (kr_ref, kmr_ref, vr_ref, dkr_ref, dvr_ref))
    found = [
        attend_back_part(
            q_ref[0], qm_ref[0], g_ref[0], lse_ref.at[0], k[0], km[0], v[0], dk.at[0], dv.at[0]
        )
        for k, km, v, dk, dv in parts
    ]
    for pair, both in enumerate(zip(*found)):
        dq_ref[0, :, pair * PAIR : (pair + 1) * PAIR] = (sum(both) * SCALE).T.astype(BF16)


def attend_back(q, qm, o, g, lse, own, rem):
    seqs, length, features = q.shape
    delta = (g.astype(F32) * o.astype(F32)).reshape(seqs, length, features // PAIR, 2, HEAD).sum(-1)
    lse = lax.dynamic_update_slice(lse, jnp.transpose(delta, (0, 2, 3, 1)), (0, 0, 2, 0))
    lanes = math.gcd(features, 2 * PAIR)
    other = rem[0].shape[1]
    own_spec, rem_spec = pair_spec(length, lanes), pair_spec(other, lanes)
    return pl.pallas_call(
        attend_back_kernel,
        grid=(seqs, features // lanes),
        in_specs=[own_spec, mask_spec(length), own_spec, lse_spec(length, lanes)]
        + [own_spec, mask_spec(length), own_spec]
        + [rem_spec, mask_spec(other), rem_spec],
        out_specs=[own_spec] * 3 + [rem_spec] * 2,
        out_shape=[jax.ShapeDtypeStruct(q.shape, BF16)] * 3
        + [jax.ShapeDtypeStruct(rem[0].shape, BF16)] * 2,
        compiler_params=params(60),
        cost_estimate=cost(
            40 * q.size * (length + other), 2 * q.size * 14, q.size * (length + other) // HEAD
        ),
        name="attend_back",
    )(q, qm, g, lse, *own, *rem)


def gelu_and_slope(x):
    bell = jnp.exp2(x * x * (-0.5 * math.log2(math.e)))
    below = 1.0 + (0.3275911 / math.sqrt(2.0)) * jnp.abs(x)
    t = pl.reciprocal(below, approx=True)
    t = t * (2.0 - below * t)
    poly = 1.061405429 * t - 1.453152027
    poly = poly * t + 1.421413741
    poly = poly * t - 0.284496736
    poly = poly * t + 0.254829592
    tail = (0.5 * poly) * t * bell
    share = jnp.where(x >= 0.0, 1.0 - tail, tail)
    return x * share, share + x * bell * (1.0 / math.sqrt(2.0 * math.pi))


def mean(values):
    return jnp.sum(values, axis=-1, keepdims=True) * (1.0 / values.shape[-1])


def norm_parts(values):
    centred = values - mean(values)
    scale = lax.rsqrt(mean(centred * centred) + EPSILON)
    return centred * scale, scale


def norm_back(upper, normed, scale):
    return scale * (upper - mean(upper) - normed * mean(upper * normed))


def column_sum(values):
    return jnp.sum(values, axis=0, keepdims=True)


def feed_kernel(layout, tok_ref, att_ref, cot_ref, vec_ref, bu_ref, wo_ref, wu_ref, wd_ref,
                out_ref, bg_ref, ag_ref, vg_ref, dbu_ref, dwu_ref, dwd_ref, dwo_ref,
                act_s, din_s, first_t, feed_t, att_t, bg_s):
    tiles, ff_steps, chunk, wide, narrow = layout
    step = pl.program_id(0)
    tile = tok_ref.shape[0]
    hidden = act_s.shape[1]
    vec = [vec_ref[i : i + 1] for i in range(6)]
    out_bias, gain_one, shift_one, down_bias, gain_two, shift_two = vec

    @pl.when(step == 0)
    def _():
        vg_ref[...] = jnp.zeros_like(vg_ref)
        dbu_ref[...] = jnp.zeros_like(dbu_ref)

    @pl.when(step < tiles)
    def _():
        start = pl.multiple_of(step * tile, tile)
        rows = pl.ds(start, tile)
        att = att_ref[...]
        normed_one, scale_one = norm_parts(
            tok_ref[...].astype(F32) + (dot(att, wo_ref[...]) + out_bias)
        )
        first = normed_one * gain_one + shift_one
        first_low = first.astype(BF16)
        first_t[:, rows] = first_low.T
        att_t[:, rows] = att.T
        feed = jnp.zeros_like(first) + down_bias
        spans = [slice(c, c + chunk) for c in range(0, hidden, chunk)]
        ahead = dot(first_low, wu_ref[:, spans[0]])
        for i, cols in enumerate(spans):
            inner = ahead + bu_ref[:, cols]
            if i + 1 < len(spans):
                ahead = dot(first_low, wu_ref[:, spans[i + 1]])
            active, slope = gelu_and_slope(inner)
            active = active.astype(BF16)
            act_s[rows, cols] = active
            din_s[rows, cols] = slope.astype(BF16)
            feed += dot(active, wd_ref[cols])
        normed_two, scale_two = norm_parts(first + feed)
        out_ref[...] = (normed_two * gain_two + shift_two).astype(BF16)
        cot = cot_ref[...].astype(F32)
        second = norm_back(cot * gain_two, normed_two, scale_two)
        feed_low = second.astype(BF16)
        feed_t[:, rows] = feed_low.T
        back = second
        ahead = dot(feed_low, wd_ref[spans[0]], NT)
        for i, cols in enumerate(spans):
            inner = ahead
            if i + 1 < len(spans):
                ahead = dot(feed_low, wd_ref[spans[i + 1]], NT)
            inner = (inner * din_s[rows, cols].astype(F32)).astype(BF16)
            din_s[rows, cols] = inner
            dbu_ref[:, cols] += column_sum(inner.astype(F32))
            back += dot(inner, wu_ref[:, cols], NT)
        residual = norm_back(back * gain_one, normed_one, scale_one)
        branch_low = residual.astype(BF16)
        bg_ref[...] = branch_low
        bg_s[rows] = branch_low
        ag_ref[...] = dot(branch_low, wo_ref[...], NT).astype(BF16)
        for i, values in enumerate(
            (
                branch_low.astype(F32),
                back * normed_one,
                back,
                feed_low.astype(F32),
                cot * normed_two,
                cot,
            )
        ):
            vg_ref[i : i + 1] += column_sum(values)

    @pl.when((step >= tiles) & (step < tiles + ff_steps))
    def _():
        cols = pl.ds(pl.multiple_of((step - tiles) * wide, wide), wide)
        dwu = dot(first_t[...], din_s[:, cols]).astype(BF16)
        dwu_ref[...] = dwu.reshape(dwu_ref.shape)
        dwd_ref[...] = dot(feed_t[...], act_s[:, cols]).astype(BF16).T

    @pl.when(step >= tiles + ff_steps)
    def _():
        cols = pl.ds(pl.multiple_of((step - tiles - ff_steps) * narrow, narrow), narrow)
        dwo_ref[...] = dot(att_t[...], bg_s[:, cols]).astype(BF16)


def feed_both_ways(tokens, attended, cotangent, vectors, up_bias, wo, wu, wd, groups):
    rows, features = tokens.shape
    hidden = wu.shape[1]
    tile = math.gcd(rows, 256)
    tiles = rows // tile
    wide, narrow = features, math.gcd(features, 384)
    ff_steps, out_steps = hidden // wide, features // narrow
    layout = (tiles, ff_steps, math.gcd(hidden, 512), wide, narrow)
    blocked = (groups, ff_steps, features // groups, wide)
    row_spec = pl.BlockSpec((tile, features), lambda i: (jnp.minimum(i, tiles - 1), 0))

    def ff_at(i):
        return jnp.clip(i - tiles, 0, ff_steps - 1)

    return pl.pallas_call(
        functools.partial(feed_kernel, layout),
        grid=(tiles + ff_steps + out_steps,),
        in_specs=[row_spec] * 3
        + [whole_spec(a.shape) for a in (vectors, up_bias, wo, wu, wd)],
        out_specs=[row_spec] * 3
        + [
            pl.BlockSpec((8, features), lambda i: (0, 0)),
            pl.BlockSpec((1, hidden), lambda i: (0, 0)),
            pl.BlockSpec((groups, 1) + blocked[2:], lambda i: (0, ff_at(i), 0, 0)),
            pl.BlockSpec((wide, features), lambda i: (ff_at(i), 0)),
            pl.BlockSpec(
                (features, narrow),
                lambda i: (0, jnp.clip(i - tiles - ff_steps, 0, out_steps - 1)),
            ),
        ],
        out_shape=[jax.ShapeDtypeStruct(tokens.shape, BF16)] * 3
        + [
            jax.ShapeDtypeStruct((8, features), F32),
            jax.ShapeDtypeStruct((1, hidden), F32),
            jax.ShapeDtypeStruct(blocked, BF16),
            jax.ShapeDtypeStruct(wd.shape, BF16),
            jax.ShapeDtypeStruct(wo.shape, BF16),
        ],
        scratch_shapes=[
            pltpu.VMEM((rows, hidden), BF16),
            pltpu.VMEM((rows, hidden), BF16),
            pltpu.VMEM((features, rows), BF16),
            pltpu.VMEM((features, rows), BF16),
            pltpu.VMEM((features, rows), BF16),
            pltpu.VMEM((rows, features), BF16),
        ],
        compiler_params=params(60),
        cost_estimate=cost(
            6 * rows * features * (features + 2 * hidden),
            2 * (6 * rows * features + 4 * features * hidden + 2 * features * features),
            2 * rows * hidden,
        ),
        name="feed_both_ways",
    )(tokens, attended, cotangent, vectors, up_bias, wo, wu, wd)


def spread(row):
    return jnp.broadcast_to(row, (PAIR, row.shape[1])).T


def as_row(ref):
    return ref[...].astype(F32).reshape(1, ref.shape[0])


def front_kernel(tokens_ref, group_ref, valid_ref, cot_ref, bq_ref, bv_ref, bo_ref, g1_ref, s1_ref, bd_ref,
                 g2_ref, s2_ref, bu_in, wq_any, wk_any, wv_any, wo_any, wu_any, wd_any,
                 out_ref, bg_ref, ag_ref, att_ref, lse_ref, qm_ref, km_ref,
                 first_t, feed_t, vg_ref, dbu_ref, q_any, k_any, v_any, rem_any, act_any, din_any,
                 wq, wk, wv, wo, wu, wd, tok_s, q_s, k_s, v_s, kr_s, vr_s, rem_s, own_codes, code_s, act_s, din_s,
                 bu_ref, weight_sem, out_sem, send_sem, recv_sem):
    s = pl.program_id(0)
    seqs = tok_s.shape[0]
    length, features = tok_s.shape[1:]
    hidden = act_s.shape[1]
    side = lax.axis_index("blk")
    other = {"blk": 1 - side}
    query_bias, value_bias, out_bias, gain_one, shift_one, down_bias, gain_two, shift_two = [
        as_row(ref) for ref in (bq_ref, bv_ref, bo_ref, g1_ref, s1_ref, bd_ref, g2_ref, s2_ref)
    ]
    pairs_of = [(wq_any, wq), (wk_any, wk), (wv_any, wv), (wo_any, wo), (wu_any, wu), (wd_any, wd)]

    def weight(i):
        return pltpu.make_async_copy(*pairs_of[i], weight_sem.at[i])

    def remote(source, target, at):
        return pltpu.make_async_remote_copy(
            src_ref=source,
            dst_ref=target,
            send_sem=send_sem.at[at],
            recv_sem=recv_sem.at[at],
            device_id=other,
            device_id_type=pl.DeviceIdType.MESH,
        )

    def exchange(at):
        return remote(tokens_ref.at[at], rem_s.at[at], at)

    def code_exchange():
        return remote(own_codes, code_s, seqs)

    def whole_out(i):
        source, target = ((q_s, q_any), (k_s, k_any.at[0]), (v_s, v_any.at[0]))[i]
        return pltpu.make_async_copy(source, target, out_sem.at[i])

    def part_out(i, at):
        source, target = (
            (kr_s, k_any.at[1, at]),
            (vr_s, v_any.at[1, at]),
            (rem_s.at[at], rem_any.at[at]),
            (act_s, act_any.at[at]),
            (din_s, din_any.at[at]),
        )[i]
        return pltpu.make_async_copy(source, target, out_sem.at[3 + i])

    @pl.when(s == 0)
    def _():
        barrier = pltpu.get_barrier_semaphore()
        pl.semaphore_signal(barrier, inc=1, device_id=other, device_id_type=pl.DeviceIdType.MESH)
        load = pltpu.make_async_copy(tokens_ref, tok_s, weight_sem.at[len(pairs_of)])
        load.start()
        for i in range(3):
            weight(i).start()
        codes = jnp.where(valid_ref[...] == 1, group_ref[...], -1).astype(F32)
        own_codes[...] = jnp.zeros_like(own_codes)
        own_codes[0:seqs] = codes
        pl.semaphore_wait(barrier, 1)
        exchange(0).start()
        code_exchange().start()
        for i in range(3, len(pairs_of)):
            weight(i).start()
        vg_ref[...] = jnp.zeros_like(vg_ref)
        dbu_ref[...] = jnp.zeros_like(dbu_ref)
        bu_ref[...] = as_row(bu_in)
        load.wait()
        for i in range(3):
            weight(i).wait()

        def project_own(at, carry):
            x = tok_s[at]
            q_s[at] = ((dot(x, wq[...]) + query_bias) * EXPO).astype(BF16)
            k_s[at] = dot(x, wk[...]).astype(BF16)
            v_s[at] = (dot(x, wv[...]) + value_bias).astype(BF16)
            return carry

        lax.fori_loop(0, seqs, project_own, 0)
        for i in range(3):
            whole_out(i).start()
        for i in range(3, len(pairs_of)):
            weight(i).wait()
        code_exchange().wait_recv()
        exchange(0).wait_send()
        if seqs > 1:
            exchange(1).start()

    for at in range(seqs):

        @pl.when(s == at)
        def _(at=at):
            exchange(at).wait_recv()
            if at:
                for i in range(3):
                    part_out(i, at - 1).wait()

    x = rem_s[s]
    kr_s[...] = dot(x, wk[...]).astype(BF16)
    vr_s[...] = (dot(x, wv[...]) + value_bias).astype(BF16)
    slot = lax.broadcasted_iota(jnp.int32, (1, PAIR), 1) % HEAD
    slot = slot.astype(F32)
    groups_row = group_ref[pl.ds(s, 1)].astype(F32)
    qm_ref[0] = jnp.where(spread(groups_row) == slot, 1.0, 0.0).astype(BF16)
    km_ref[0, 0] = jnp.where(spread(own_codes[pl.ds(s, 1)]) == slot, 0.0, MASKED).astype(BF16)
    km_ref[1, 0] = jnp.where(spread(code_s[pl.ds(s, 1)]) == slot, 0.0, MASKED).astype(BF16)
    for at in range(seqs):

        @pl.when(s == at)
        def _(at=at):
            for i in range(3):
                part_out(i, at).start()

    groups = features // (2 * PAIR)

    def heads(group, carry):
        lanes = pl.ds(pl.multiple_of(group * 2 * PAIR, 2 * PAIR), 2 * PAIR)
        attend_group(
            q_s[s, :, lanes],
            qm_ref[0],
            [(k_s[s, :, lanes], km_ref[0, 0], v_s[s, :, lanes]), (kr_s[:, lanes], km_ref[1, 0], vr_s[:, lanes])],
            att_ref.at[0, :, lanes],
            lse_ref.at[0, pl.ds(group * 2, 2)],
        )
        return carry

    lax.fori_loop(0, groups, heads, 0)

    for at in range(1, seqs):

        @pl.when(s == at)
        def _(at=at):
            for i in range(3, 5):
                part_out(i, at - 1).wait()

    tile = math.gcd(length, FEED_ROWS)
    chunk = math.gcd(hidden, 1024)
    spans = [slice(c, c + chunk) for c in range(0, hidden, chunk)]

    def feed_rows(t, carry):
        rows = pl.ds(pl.multiple_of(t * tile, tile), tile)
        att = att_ref[0, rows]
        normed_one, scale_one = norm_parts(
            tok_s[s, rows].astype(F32) + (dot(att, wo[...]) + out_bias)
        )
        first = normed_one * gain_one + shift_one
        first_low = first.astype(BF16)
        first_t[:, rows] = first_low.T
        feed = jnp.zeros_like(first) + down_bias
        ahead = dot(first_low, wu[:, spans[0]])
        for i, cols in enumerate(spans):
            inner = ahead + bu_ref[:, cols]
            if i + 1 < len(spans):
                ahead = dot(first_low, wu[:, spans[i + 1]])
            active, slope = gelu_and_slope(inner)
            active = active.astype(BF16)
            act_s[rows, cols] = active
            din_s[rows, cols] = slope.astype(BF16)
            feed += dot(active, wd[cols])
        normed_two, scale_two = norm_parts(first + feed)
        out_ref[0, rows] = (normed_two * gain_two + shift_two).astype(BF16)
        cot = cot_ref[0, rows].astype(F32)
        second = norm_back(cot * gain_two, normed_two, scale_two)
        feed_low = second.astype(BF16)
        feed_t[:, rows] = feed_low.T
        back = second
        ahead = dot(feed_low, wd[spans[0]], NT)
        for i, cols in enumerate(spans):
            inner = ahead
            if i + 1 < len(spans):
                ahead = dot(feed_low, wd[spans[i + 1]], NT)
            inner = (inner * din_s[rows, cols].astype(F32)).astype(BF16)
            din_s[rows, cols] = inner
            dbu_ref[:, cols] += column_sum(inner.astype(F32))
            back += dot(inner, wu[:, cols], NT)
        residual = norm_back(back * gain_one, normed_one, scale_one)
        branch_low = residual.astype(BF16)
        bg_ref[0, rows] = branch_low
        att_grad = dot(branch_low, wo[...], NT).astype(BF16)
        ag_ref[0, rows] = att_grad
        product = att_grad.astype(F32) * att.astype(F32)
        coarse = product.astype(BF16)
        fine = (product - coarse.astype(F32)).astype(BF16)
        heads_count = features // HEAD
        of_head = lax.broadcasted_iota(jnp.int32, (heads_count, features), 1) // HEAD
        selector = (of_head == lax.broadcasted_iota(jnp.int32, of_head.shape, 0)).astype(F32)
        selector = selector.astype(BF16)
        delta = dot(selector, coarse, NT) + dot(selector, fine, NT)
        for pair in range(features // PAIR):
            lse_ref[0, pair, 2:4, rows] = delta[2 * pair : 2 * pair + 2]
        for i, values in enumerate(
            (
                branch_low.astype(F32),
                back * normed_one,
                back,
                feed_low.astype(F32),
                cot * normed_two,
                cot,
            )
        ):
            vg_ref[i : i + 1] += column_sum(values)
        return carry

    lax.fori_loop(0, length // tile, feed_rows, 0)

    for at in range(seqs):

        @pl.when(s == at)
        def _(at=at):
            for i in range(3, 5):
                part_out(i, at).start()
            if at < seqs - 1:
                exchange(at + 1).wait_send()
            if at + 2 < seqs:
                exchange(at + 2).start()
            if at == seqs - 1:
                for i in range(3):
                    whole_out(i).wait()
                for i in range(5):
                    part_out(i, at).wait()
                code_exchange().wait_send()


def front(tokens, group_ids, valid, cotangent, vectors, up_bias, weights):
    seqs, length, features = tokens.shape
    hidden = up_bias.shape[0]
    pairs = features // PAIR
    anywhere = pl.BlockSpec(memory_space=pl.ANY)

    def at_seq(*shape):
        return pl.BlockSpec((1,) + shape, lambda s: (s,) + (0,) * len(shape))

    def of_seqs(*shape, dtype=BF16):
        return jax.ShapeDtypeStruct((seqs,) + shape, dtype)

    def fixed(*shape):
        return pl.BlockSpec(shape, lambda s: (0,) * len(shape))

    rows, mask, lses, wide = (length, features), (length, PAIR), (pairs, 8, length), (length, hidden)
    turned = pl.BlockSpec((features, length), lambda s: (0, s))
    return pl.pallas_call(
        front_kernel,
        grid=(seqs,),
        in_specs=[anywhere, whole_spec(group_ids.shape), whole_spec(valid.shape), at_seq(*rows)]
        + [whole_spec(v.shape) for v in vectors + (up_bias,)]
        + [anywhere] * 6,
        out_specs=[at_seq(*rows)] * 4
        + [at_seq(*lses), at_seq(*mask)]
        + [pl.BlockSpec((2, 1) + mask, lambda s: (0, s, 0, 0))]
        + [turned] * 2
        + [fixed(8, features), fixed(1, hidden)]
        + [anywhere] * 6,
        out_shape=[of_seqs(*rows)] * 4
        + [of_seqs(*lses, dtype=F32), of_seqs(*mask)]
        + [jax.ShapeDtypeStruct((2, seqs) + mask, BF16)]
        + [jax.ShapeDtypeStruct((features, seqs * length), BF16)] * 2
        + [jax.ShapeDtypeStruct((8, features), F32), jax.ShapeDtypeStruct((1, hidden), F32)]
        + [of_seqs(*rows)]
        + [jax.ShapeDtypeStruct((2, seqs) + rows, BF16)] * 2
        + [of_seqs(*rows)]
        + [of_seqs(*wide)] * 2,
        scratch_shapes=[pltpu.VMEM(w.shape, BF16) for w in weights]
        + [pltpu.VMEM(tokens.shape, BF16)] * 4
        + [pltpu.VMEM(rows, BF16)] * 2
        + [pltpu.VMEM(tokens.shape, BF16)]
        + [pltpu.VMEM((seqs + -seqs % 8, length), F32)] * 2
        + [pltpu.VMEM(wide, BF16)] * 2
        + [pltpu.VMEM((1, hidden), F32)]
        + [pltpu.SemaphoreType.DMA((7,)), pltpu.SemaphoreType.DMA((8,))]
        + [pltpu.SemaphoreType.DMA((seqs + 1,))] * 2,
        compiler_params=pltpu.CompilerParams(
            collective_id=2, has_side_effects=True, vmem_limit_bytes=63 * MIB
        ),
        cost_estimate=cost(
            2 * tokens.size * (9 * features + 4 * hidden + 8 * length), 2 * 20 * tokens.size, tokens.size * 24
        ),
        name="front",
    )(tokens, group_ids, valid, cotangent, *vectors, up_bias, *weights)


def feed_weights_kernel(blocks, first_ref, din_ref, feed_ref, act_ref, att_any, bg_any,
                        dwu_ref, dwd_ref, dwo_ref, up_s, up_in, down_s, down_in, out_s, out_in,
                        att_s, bg_s, near_sem, send_sem, recv_sem):
    step = pl.program_id(0)
    features = first_ref.shape[0]
    me = lax.axis_index("dp")
    core = me % 2
    other = {"dp": me + 1 - 2 * core}

    def loads():
        return [
            pltpu.make_async_copy(att_any, att_s, near_sem.at[0]),
            pltpu.make_async_copy(bg_any, bg_s, near_sem.at[1]),
        ]

    each, deep = down_in.shape[1:3]

    def piece(i, side):
        return pl.ds(pl.multiple_of((2 * i + side) * deep, 16), deep)

    def swaps(block):
        if block == blocks:
            pairs = [(out_s.at[:, 1 - core], out_in)]
        else:
            pairs = [(up_s.at[block % 2, :, 1 - core], up_in.at[block])]
            for i in range(each):
                pairs.append((down_s.at[block % 2, piece(i, 1 - core)], down_in.at[block, i]))
        return [
            pltpu.make_async_remote_copy(
                src_ref=source,
                dst_ref=target,
                send_sem=send_sem.at[(each + 1) * block + i],
                recv_sem=recv_sem.at[(each + 1) * block + i],
                device_id=other,
                device_id_type=pl.DeviceIdType.MESH,
            )
            for i, (source, target) in enumerate(pairs)
        ]

    @pl.when(step == 0)
    def _():
        for load in loads():
            load.start()
        barrier = pltpu.get_barrier_semaphore()
        pl.semaphore_signal(barrier, inc=1, device_id=other, device_id_type=pl.DeviceIdType.MESH)
        pl.semaphore_wait(barrier, 1)

    @pl.when(step < blocks)
    def _():
        slot = step % 2
        tile = math.gcd(features, 256)
        for start in range(0, features, tile):
            cols = slice(start, start + tile)
            up = dot(first_ref[...], din_ref[:, cols]).astype(BF16)
            up_s[slot, :, :, :, cols] = up.reshape(up_s.shape[1:4] + (tile,))
            down_s[slot, cols] = dot(feed_ref[...], act_ref[:, cols]).astype(BF16).T

    for block in range(blocks):

        @pl.when(step == block)
        def _(block=block):
            for swap in swaps(block):
                swap.start()

    @pl.when(step == blocks)
    def _():
        for load in loads():
            load.wait()
        out_s[...] = dot(att_s[...].T, bg_s[...]).astype(BF16).reshape(out_s.shape)
        for swap in swaps(blocks):
            swap.start()

    for block in range(blocks):

        @pl.when(step == block + 1)
        def _(block=block):
            for swap in swaps(block):
                swap.wait()
            dwu_ref[:, 0] = (up_s[block % 2, :, core].astype(F32) + up_in[block].astype(F32)).astype(BF16)
            for i in range(each):
                mine = down_s[block % 2, piece(i, core)].astype(F32)
                dwd_ref[i] = (mine + down_in[block, i].astype(F32)).astype(BF16)

    @pl.when(step == blocks + 1)
    def _():
        for swap in swaps(blocks):
            swap.wait()
        dwo_ref[...] = (out_s[:, core].astype(F32) + out_in[...].astype(F32)).astype(BF16)


def feed_weights(first_t, din, feed_t, act, att, bg):
    dp = lax.axis_size("dp")
    features, rows = first_t.shape
    hidden = act.shape[1]
    blocks, half, low, deep = hidden // features, dp // 2, features // dp, hidden // dp
    each = half // blocks
    wide_spec = pl.BlockSpec((rows, features), lambda i: (0, jnp.minimum(i, blocks - 1)))
    anywhere = pl.BlockSpec(memory_space=pl.ANY)

    def behind(i):
        return jnp.clip(i - 1, 0, blocks - 1)

    return pl.pallas_call(
        functools.partial(feed_weights_kernel, blocks),
        grid=(blocks + 2,),
        in_specs=[
            whole_spec(first_t.shape),
            wide_spec,
            whole_spec(feed_t.shape),
            wide_spec,
            anywhere,
            anywhere,
        ],
        out_specs=[
            pl.BlockSpec((half, 1, low, features), lambda i: (0, behind(i), 0, 0)),
            pl.BlockSpec((each, deep, features), lambda i: (behind(i), 0, 0)),
            pl.BlockSpec((half, low, features), lambda i: (0, 0, 0)),
        ],
        out_shape=[
            jax.ShapeDtypeStruct((half, blocks, low, features), BF16),
            jax.ShapeDtypeStruct((half, deep, features), BF16),
            jax.ShapeDtypeStruct((half, low, features), BF16),
        ],
        scratch_shapes=[
            pltpu.VMEM((2, half, 2, low, features), BF16),
            pltpu.VMEM((blocks, half, low, features), BF16),
            pltpu.VMEM((2, features, features), BF16),
            pltpu.VMEM((blocks, each, deep, features), BF16),
            pltpu.VMEM((half, 2, low, features), BF16),
            pltpu.VMEM((half, low, features), BF16),
            pltpu.VMEM(att.shape, BF16),
            pltpu.VMEM(bg.shape, BF16),
            pltpu.SemaphoreType.DMA((2,)),
            pltpu.SemaphoreType.DMA(((each + 1) * blocks + 1,)),
            pltpu.SemaphoreType.DMA(((each + 1) * blocks + 1,)),
        ],
        compiler_params=pltpu.CompilerParams(
            collective_id=3, has_side_effects=True, vmem_limit_bytes=63 * MIB
        ),
        cost_estimate=cost(
            2 * rows * features * (2 * hidden + features), 4 * rows * (hidden + 2 * features)
        ),
        name="feed_weights",
    )(first_t, din, feed_t, act, att, bg)


def own_back_kernel(bg_ref, dq_ref, dk_ref, dv_ref, wq_ref, wk_ref, wv_ref, out_ref):
    total = bg_ref[0].astype(F32) + dot(dq_ref[0], wq_ref[...], NT)
    total += dot(dk_ref[0], wk_ref[...], NT)
    total += dot(dv_ref[0], wv_ref[...], NT)
    out_ref[0] = total.astype(BF16)


def rem_back_kernel(dk_ref, dv_ref, wk_ref, wv_ref, out_ref):
    total = dot(dk_ref[0], wk_ref[...], NT) + dot(dv_ref[0], wv_ref[...], NT)
    out_ref[0] = total.astype(BF16)


def tokens_back(kernel, rows, weights):
    seqs, length, features = rows[0].shape
    tile = math.gcd(length, 512)
    row_spec = pl.BlockSpec((1, tile, features), lambda s, i: (s, i, 0))
    size = rows[0].size
    return pl.pallas_call(
        kernel,
        grid=(seqs, length // tile),
        in_specs=[row_spec] * len(rows) + [whole_spec(w.shape) for w in weights],
        out_specs=row_spec,
        out_shape=jax.ShapeDtypeStruct(rows[0].shape, BF16),
        compiler_params=params(60),
        cost_estimate=cost(2 * size * features * len(weights), 2 * size * (1 + len(rows))),
        name="tokens_back",
    )(*rows, *weights)


def weights_back_kernel(tok_ref, rem_ref, dq_ref, dko_ref, dvo_ref, dkr_ref, dvr_ref,
                        wq_ref, wk_ref, wv_ref, bq_ref, bv_ref, tok_t, rem_t):
    @pl.when(pl.program_id(0) == 0)
    def _():
        tok_t[...] = tok_ref[...].T
        rem_t[...] = rem_ref[...].T

    wq_ref[...] = dot(tok_t[...], dq_ref[...]).astype(BF16)
    wk_ref[...] = (dot(tok_t[...], dko_ref[...]) + dot(rem_t[...], dkr_ref[...])).astype(BF16)
    wv_ref[...] = (dot(tok_t[...], dvo_ref[...]) + dot(rem_t[...], dvr_ref[...])).astype(BF16)
    bq_ref[...] = column_sum(dq_ref[...].astype(F32))
    bv_ref[...] = column_sum(dvo_ref[...].astype(F32)) + column_sum(dvr_ref[...].astype(F32))


def weights_back(tok, rem, dq, dko, dvo, dkr, dvr):
    rows, features = tok.shape
    others = rem.shape[0]
    wide = math.gcd(features, 256)
    own_spec = pl.BlockSpec((rows, wide), lambda j: (0, j))
    rem_spec = pl.BlockSpec((others, wide), lambda j: (0, j))
    bias_spec = pl.BlockSpec((1, wide), lambda j: (0, j))
    return pl.pallas_call(
        weights_back_kernel,
        grid=(features // wide,),
        in_specs=[
            whole_spec(tok.shape),
            whole_spec(rem.shape),
            own_spec,
            own_spec,
            own_spec,
            rem_spec,
            rem_spec,
        ],
        out_specs=[pl.BlockSpec((features, wide), lambda j: (0, j))] * 3 + [bias_spec] * 2,
        out_shape=[jax.ShapeDtypeStruct((features, features), BF16)] * 3
        + [jax.ShapeDtypeStruct((1, features), F32)] * 2,
        scratch_shapes=[
            pltpu.VMEM((features, rows), BF16),
            pltpu.VMEM((features, others), BF16),
        ],
        compiler_params=params(60),
        cost_estimate=cost(
            2 * features * features * (3 * rows + 2 * others),
            2 * (4 * tok.size + 3 * rem.size + 3 * features * features),
        ),
        name="weights_back",
    )(tok, rem, dq, dko, dvo, dkr, dvr)


def halve(value, axis, bit):
    size = lax.axis_size(axis)
    mine = (lax.axis_index(axis) >> bit) & 1
    pairs = value.reshape((value.shape[0] // 2, 2) + value.shape[1:])
    keep = lax.dynamic_index_in_dim(pairs, mine, 1, keepdims=False)
    send = lax.dynamic_index_in_dim(pairs, 1 - mine, 1, keepdims=False)
    came = lax.ppermute(send, axis, [(i, i ^ (1 << bit)) for i in range(size)])
    return keep.astype(F32) + came.astype(F32)


def scatter_sum(value, low=True):
    dp, blk = lax.axis_size("dp"), lax.axis_size("blk")
    if dp & (dp - 1) or blk & (blk - 1):
        return lax.psum_scatter(
            value.astype(F32), ("dp", "blk"), scatter_dimension=0, tiled=True
        )
    kept = value.dtype
    each = value.shape[0] // (dp * blk)
    value = value.reshape((dp, blk * each) + value.shape[1:])
    for bit in range(dp.bit_length() - 1):
        value = halve(value, "dp", bit).astype(kept)
    value = value.reshape((blk, each) + value.shape[2:])
    for bit in range(blk.bit_length() - 1):
        value = halve(value, "blk", bit)
        value = value if (2 << bit) == blk else value.astype(kept)
    return value.reshape(value.shape[1:]).astype(F32)


class Unit:
    def __init__(self, parts, rows, columns, halves, outs):
        self.parts, self.rows, self.columns = parts, rows, columns
        self.halves, self.outs = halves, outs
        self.first = 1 if parts else 0
        self.half = rows // (2 * halves)
        self.last_type = BF16 if (rows // 2) % 16 == 0 else F32


def timetable(units, bits, seqs, groups, slot_us, token_us):
    free, pending, table = {}, [], []
    slots = seqs * groups * 2

    def launch(key, now):
        kind, which, step = key
        if kind == "tokens":
            link, us = "blk", token_us
        elif kind == "vectors":
            link, us = None, 1.0
        else:
            us = units[which].rows * units[which].columns * 2e-5
            us *= 1 << max(bits - 1 - step, 0)
            us *= {0: 0.4, bits - 1: 3.0}.get(step, 1.2)
            link = {0: "core", bits - 1: "far", bits: "blk"}.get(step, "near")
        start = max(now, free.get(link, 0.0))
        if link:
            free[link] = start + us
        if kind != "tokens":
            pending.append((start + us + 2.5, key))

    for u, unit in enumerate(units):
        if unit.parts:
            launch(("unit", u, 1), 3.0)
    first_group = sum(1 for unit in units if unit.parts)
    now = 0.0
    while len(table) < slots or pending:
        slot = len(table)
        if slot < slots:
            now = (slot + 1) * slot_us
            part, major, minor = slot // (seqs * groups), slot // groups % seqs, slot % groups
            if part == 0 and minor == groups - 1:
                launch(("tokens", major, 0), now)
            major, minor = divmod(slot - seqs * groups, seqs)
            if part == 1 and minor == seqs - 1:
                launch(("unit", first_group + major, 0), now)
            if slot == slots - 1:
                launch(("vectors", 0, 0), now)
            due = sorted(p for p in pending if p[0] <= now)
        else:
            due = [min(pending)]
            now = max(now + 0.3, due[0][0])
        table.append([key for _, key in due])
        for found in due:
            pending.remove(found)
            kind, which, step = found[1]
            if step < bits:
                launch((kind, which, step + 1), now)
    tail = [key for keys in table[slots:] for key in keys]
    return table[:slots], tail + [("tokens", s, 0) for s in range(seqs)]


def order_of(step, seqs, groups):
    part = step // (seqs * groups)
    left = step - part * (seqs * groups)
    s = left // groups * (1 - part) + left % seqs * part
    h = left % groups * (1 - part) + left // seqs * part
    return part, s, h


def back_kernel(units, bits, groups, table, tail, n_out, *refs):
    (q_ref, qm_ref, g_ref, lse_ref, k_ref, km_ref, v_ref,
     tok_ref, rem_ref, wq_ref, wk_ref, wv_ref, vg_ref, vu_ref) = refs[:14]
    sources, refs = refs[14:17], list(refs[17:])
    tokens_any, rem_in, *outs = refs[:n_out]
    refs = refs[n_out:]
    kept = [refs.pop(0) for _ in units]
    landed = [
        [refs.pop(0) if k >= unit.first else None for k in range(bits)] for unit in units
    ]
    wide = [refs.pop(0) for _ in units]
    parting = [refs.pop(0) for _ in units]
    last = [refs.pop(0) for _ in units]
    (weight_sum, group_src, total_s, turned, dq_part, dq_s, dk_s, dv_s,
     rem_out, vec, vec_in, bias_sum, send_sem, recv_sem, local_sem, out_sem) = refs
    step = pl.program_id(0)
    steps = pl.num_programs(0)
    seqs = rem_out.shape[0]
    part, s, h = order_of(step, seqs, groups)
    features = tok_ref.shape[2]
    me, side = lax.axis_index("dp"), lax.axis_index("blk")
    core = me % 2

    def swapped(k):
        return {1: 2, 2: 1}.get(k, k) if bits > 2 else k

    def pick(values, k):
        return values[k] + (values[swapped(k)] - values[k]) * core

    bit_own = [(me // (1 << bit)) % 2 for bit in range(bits)]
    across = [me + (1 << bit) * (1 - 2 * bit_own[bit]) for bit in range(bits)]
    own = [pick(bit_own, k) for k in range(bits)]
    partner = [{"dp": pick(across, k)} for k in range(bits)] + [{"blk": 1 - side}]
    first_group = sum(1 for unit in units if unit.parts)
    lead = (slice(None),) * (bits - 1)

    def natural(digits):
        by_step = [None] + list(digits[::-1])
        return tuple(
            by_step[bit] if swapped(bit) == bit else pick(by_step, bit) for bit in range(bits - 1, 0, -1)
        )

    def digits_of(n, count):
        return [(n // (1 << (count - 1 - i))) % 2 for i in range(count)]

    sems = {}
    for u, unit in enumerate(units):
        for k in range(unit.first, bits + 1):
            sems["unit", u, k, 0] = len(sems)
    for k in range(bits + 1):
        sems["vectors", 0, k, 0] = len(sems)
    for k in range(seqs):
        sems["tokens", k, 0, 0] = len(sems)

    def remote(source, target, device, key):
        return pltpu.make_async_remote_copy(
            src_ref=source,
            dst_ref=target,
            send_sem=send_sem.at[sems[key]],
            recv_sem=recv_sem.at[sems[key]],
            device_id=device,
            device_id_type=pl.DeviceIdType.MESH,
        )

    near_sems = {}
    for u, unit in enumerate(units):
        for p in range(len(unit.parts or ())):
            for n in range(1 << min(bits - 1, 2)):
                near_sems[u, p, n] = len(near_sems)

    def spot(k, value):
        return tuple(
            own[at] if at < k else value if at == k else slice(None) for at in range(bits - 1, 0, -1)
        )

    def copies(kind, which, k):
        if kind == "tokens":
            return [remote(rem_out.at[which], rem_in.at[which], partner[bits], (kind, which, 0, 0))]
        if kind == "vectors":
            return [remote(vec.at[k], vec_in.at[k], partner[k], (kind, 0, k, 0))]
        u, unit = which, units[which]
        if k == bits:
            return [remote(parting[u], last[u], partner[bits], (kind, u, k, 0))]
        if k:
            source = kept[u].at[spot(k, 1 - own[k])]
            return [remote(source, landed[u][k], partner[k], (kind, u, k, 0))]
        source = group_src.at[(u - first_group,) + lead + (1 - core,)]
        return [remote(source, landed[u][0], partner[0], (kind, u, 0, 0))]

    def near_copies(u):
        found, row = [], 0
        for p, (source, first, rows) in enumerate(units[u].parts):
            for n in range(1 << min(bits - 1, 2)):
                digits = digits_of(n, min(bits - 1, 2))
                digits = [slice(None)] * (bits - 1 - len(digits)) + digits
                found.append(
                    pltpu.make_async_copy(
                        sources[source].at[natural(digits) + (pl.ds(first, rows),)],
                        kept[u].at[tuple(digits) + (pl.ds(row, rows),)],
                        local_sem.at[near_sems[u, p, n]],
                    )
                )
            row += rows
        return found

    def launch(*key):
        for copy in copies(*key):
            copy.start()

    def halves_of(u, which):
        unit = units[u]
        return [
            wide[u][pl.ds(pl.multiple_of(i * 2 * unit.half + which * unit.half, 8), unit.half)]
            for i in range(unit.halves)
        ]

    def receive(kind, which, k):
        for copy in copies(kind, which, k):
            copy.wait_recv()
        if kind == "tokens":
            return
        if kind == "vectors":
            vec[k + 1] = vec[k] + vec_in[k]
            if k < bits:
                launch(kind, 0, k + 1)
            return
        u, unit = which, units[which]
        if k == bits:
            for i, (mine, (out, rows, columns)) in enumerate(zip(halves_of(u, side), unit.outs)):
                came = last[u][...].astype(F32)[i * unit.half : (i + 1) * unit.half]
                outs[out][rows, columns] = mine + came
            return
        place = spot(k, own[k]) if k else lead
        open_at = [i for i, at in enumerate(place) if isinstance(at, slice)]

        def add(n, carry):
            at, where = list(place), digits_of(n, len(open_at))
            for i, digit in zip(open_at, where):
                at[i] = digit
            at = tuple(at)
            if k:
                mine, came = kept[u][at], landed[u][k][tuple(where)]
            else:
                mine = group_src[(u - first_group,) + natural(at) + (core,)]
                came = landed[u][0][natural(at)]
            total = mine.astype(F32) + came.astype(F32)
            if k == bits - 1:
                wide[u][...] = total
            else:
                kept[u][at] = total.astype(BF16)
            return carry

        if open_at:
            lax.fori_loop(0, 1 << len(open_at), add, 0)
        else:
            add(0, 0)
        if k == bits - 1:
            pieces = halves_of(u, 1 - side)
            pieces = pieces[0] if len(pieces) == 1 else jnp.concatenate(pieces, axis=0)
            parting[u][...] = pieces.astype(unit.last_type)
        launch(kind, u, k + 1)

    @pl.when(step == 0)
    def _():
        barrier = pltpu.get_barrier_semaphore()
        for other in partner:
            pl.semaphore_signal(barrier, inc=1, device_id=other, device_id_type=pl.DeviceIdType.MESH)
        pl.semaphore_wait(barrier, bits + 1)
        for u, unit in enumerate(units):
            if unit.parts:
                for copy in near_copies(u):
                    copy.start()
        for u, unit in enumerate(units):
            if unit.parts:
                for copy in near_copies(u):
                    copy.wait()
                launch("unit", u, 1)
        weight_sum[...] = jnp.zeros_like(weight_sum)
        bias_sum[...] = jnp.zeros_like(bias_sum)

    @pl.when((part == 0) & (h == 0))
    def _():
        turned[0] = rem_ref[0].T
        total_s[...] = jnp.zeros_like(total_s)

    @pl.when((part == 1) & (h == 0))
    def _():
        turned[s] = tok_ref[0].T

    width = q_ref.shape[2]
    columns = pl.ds(pl.multiple_of(h * width, width), width)

    found = attend_back_part(
        q_ref[0], qm_ref[0], g_ref[0], lse_ref.at[0], k_ref[0, 0], km_ref[0, 0], v_ref[0, 0],
        dk_s.at[s, :, columns], dv_s.at[s, :, columns],
    )
    dk, dv = dk_s[s, :, columns], dv_s[s, :, columns]
    x_t = turned[s * part]
    weight_sum[h, 1] += dot(x_t, dk)
    weight_sum[h, 2] += dot(x_t, dv)
    bias_sum[h, 1:2] += column_sum(dv.astype(F32))

    @pl.when(part == 0)
    def _():
        total_s[...] += dot(dk, wk_ref[:, columns], NT) + dot(dv, wv_ref[:, columns], NT)
        for pair, value in enumerate(found):
            dq_part[s, h, pair] = value.astype(dq_part.dtype)

    @pl.when(part == 1)
    def _():
        queries = []
        for pair, value in enumerate(found):
            value = (value + dq_part[s, h, pair].astype(F32)) * SCALE
            queries.append(value.T.astype(BF16))
        dq = jnp.concatenate(queries, axis=1)
        dq_s[s, :, columns] = dq
        weight_sum[h, 0] += dot(x_t, dq)
        bias_sum[h, 0:1] += column_sum(dq.astype(F32))

    for at in range(seqs):

        @pl.when(step == (at + 1) * groups - 1)
        def _(at=at):
            rem_out[at] = total_s[...].astype(BF16)
            launch("tokens", at, 0)

    for at in range(groups):

        @pl.when(step == steps - (groups - 1 - at) * seqs - 1)
        def _(at=at):
            rows = features // (1 << bits)
            for i in range(3):
                piece = weight_sum[at, i].astype(BF16)
                piece = piece.reshape((2,) * bits + (rows, piece.shape[1]))
                group_src[(at,) + (slice(None),) * bits + (slice(i * rows, (i + 1) * rows),)] = piece
            launch("unit", first_group + at, 0)

    @pl.when(step == steps - 1)
    def _():
        vec[0] = jnp.zeros_like(vec[0])
        vec[0, 0:6] = vg_ref[0:6]
        for at in range(groups):
            vec[0, 6:8, at * width : (at + 1) * width] = bias_sum[at, 0:2]
        blocks = vu_ref.shape[1] // features
        for at in range(blocks):
            vec[0, 8 + at : 9 + at] = vu_ref[:, at * features : (at + 1) * features]
        launch("vectors", 0, 0)

    for at, keys in enumerate(table):
        if keys:

            @pl.when(step == at)
            def _(keys=keys):
                for key in keys:
                    receive(*key)

    @pl.when(step == steps - 1)
    def _():
        def own_out(at):
            return pltpu.make_async_copy(dq_s.at[at], tokens_any.at[at], out_sem.at[at])

        left = list(tail)
        for at in range(seqs):
            total = dot(dq_s[at], wq_ref[...], NT)
            total += dot(dk_s[at], wk_ref[...], NT) + dot(dv_s[at], wv_ref[...], NT)
            dq_s[at] = total.astype(BF16)
            own_out(at).start()
            for _ in range(3):
                if left:
                    receive(*left.pop(0))
        for key in left:
            receive(*key)
        for at in range(seqs):
            own_out(at).wait()
        shards = (1 << bits) * 2
        place = me * 2 + side
        share = features // shards
        rows = pltpu.roll(vec[bits + 1, 0:8], (shards - place) * share % features, 1)
        outs[-1][0:8] = rows[:, :PAIR]
        share = vu_ref.shape[1] // shards
        each = features // share
        row = vec[bits + 1, pl.ds(8 + place // each, 1)]
        rows = pltpu.roll(jnp.broadcast_to(row, (8, features)), (each - place % each) * share % features, 1)
        outs[-1][8:16] = rows[:, :PAIR]
        for u, unit in enumerate(units):
            for k in range(unit.first, bits + 1):
                for copy in copies("unit", u, k):
                    copy.wait_send()
        for k in range(bits + 1):
            copies("vectors", 0, k)[0].wait_send()
        for k in range(seqs):
            copies("tokens", k, 0)[0].wait_send()


def back_and_sum(q, qm, g, lse, k, km, v, tokens, rem_tokens, weights, dwd, dwu, dwo, vg, vu):
    bits = lax.axis_size("dp").bit_length() - 1
    seqs, length, features = q.shape
    width = math.gcd(features, 2 * PAIR)
    groups, pairs = features // width, width // PAIR
    low, deep, blocks = dwo.shape[1], dwd.shape[1], dwu.shape[1]
    lead = (2,) * bits
    sources = [x.reshape(lead[1:] + (-1, features)) for x in (dwd, dwu, dwo)]
    every = slice(None)
    units = []
    quarter = deep // 4
    for i in range(2):
        at = slice(i * quarter, (i + 1) * quarter)
        parts = [(0, i * quarter, quarter), (0, (2 + i) * quarter, quarter)]
        units.append(Unit(parts, 2 * quarter, features, 1, [(0, at, every)]))
    for i in range(2):
        found = range(i * blocks // 2, (i + 1) * blocks // 2)
        units.append(
            Unit(
                [(1, found[0] * low, len(found) * low)],
                len(found) * low,
                features,
                len(found),
                [(1, every, slice(b * features, (b + 1) * features)) for b in found],
            )
        )
    units.append(Unit([(2, 0, low)], low, features, 1, [(2, every, every)]))
    for h in range(groups):
        columns = slice(h * width, (h + 1) * width)
        units.append(Unit(None, 3 * low, width, 3, [(3 + i, every, columns) for i in range(3)]))
    table, tail = timetable(units, bits, seqs, groups, 4.2, length * features * 4e-5)

    half = low // 2
    out_shape = [
        jax.ShapeDtypeStruct(q.shape, BF16),
        jax.ShapeDtypeStruct(q.shape, BF16),
        jax.ShapeDtypeStruct((deep // 2, features), F32),
        jax.ShapeDtypeStruct((half, blocks * features), F32),
        *(jax.ShapeDtypeStruct((half, features), F32) for _ in range(4)),
        jax.ShapeDtypeStruct((16, PAIR), F32),
    ]
    tops = lead[1:]
    scratch = [pltpu.VMEM(tops + (u.rows, u.columns), BF16) for u in units]
    for u in units:
        scratch += [pltpu.VMEM(tops[k:] + (u.rows, u.columns), BF16) for k in range(u.first, bits)]
    scratch += [pltpu.VMEM((u.rows, u.columns), F32) for u in units]
    scratch += [pltpu.VMEM((u.rows // 2, u.columns), u.last_type) for u in units] * 2
    count = len(units) * (bits + 1) + bits + 1 + seqs
    near = sum(len(u.parts) << min(bits - 1, 2) for u in units if u.parts)
    scratch += [
        pltpu.VMEM((groups, 3, features, width), F32),
        pltpu.VMEM((groups,) + lead + (3 * low, width), BF16),
        pltpu.VMEM((length, features), F32),
        pltpu.VMEM((seqs, features, length), BF16),
        pltpu.VMEM((seqs, groups, pairs, PAIR, length), F32),
        *(pltpu.VMEM((seqs, length, features), BF16) for _ in range(4)),
        pltpu.VMEM((bits + 2, 16, features), F32),
        pltpu.VMEM((bits + 1, 16, features), F32),
        pltpu.VMEM((groups, 8, width), F32),
        pltpu.SemaphoreType.DMA((count,)),
        pltpu.SemaphoreType.DMA((count,)),
        pltpu.SemaphoreType.DMA((near,)),
        pltpu.SemaphoreType.DMA((seqs,)),
    ]

    def at_step(shape, index):
        return pl.BlockSpec(shape, lambda i: index(*order_of(i, seqs, groups)))

    heads_at = at_step((1, length, width), lambda p, s, h: (s, 0, h))
    keys_at = at_step((1, 1, length, width), lambda p, s, h: (1 - p, s, 0, h))

    def rows_at(which):
        last = seqs - 1
        return pl.BlockSpec(
            (1, length, features),
            lambda i: (jnp.clip(i // groups if which == 0 else i - seqs * groups, 0, last), 0, 0),
            pipeline_mode=pl.Buffered(1),
        )

    def fixed(shape):
        return pl.BlockSpec(shape, lambda i: (0,) * len(shape), pipeline_mode=pl.Buffered(1))

    return pl.pallas_call(
        functools.partial(back_kernel, units, bits, groups, table, tail, len(out_shape)),
        grid=(2 * seqs * groups,),
        in_specs=[
            heads_at,
            at_step((1, length, PAIR), lambda p, s, h: (s, 0, 0)),
            heads_at,
            at_step((1, pairs, 8, length), lambda p, s, h: (s, h, 0, 0)),
            keys_at,
            at_step((1, 1, length, PAIR), lambda p, s, h: (1 - p, s, 0, 0)),
            keys_at,
            rows_at(1),
            rows_at(0),
        ]
        + [whole_spec(w.shape) for w in weights + (vg, vu)]
        + [pl.BlockSpec(memory_space=pl.ANY)] * 3,
        out_specs=[pl.BlockSpec(memory_space=pl.ANY)] * 2
        + [fixed(s.shape) for s in out_shape[2:]],
        out_shape=out_shape,
        scratch_shapes=scratch,
        compiler_params=pltpu.CompilerParams(
            collective_id=1, has_side_effects=True, vmem_limit_bytes=63 * MIB
        ),
        cost_estimate=cost(80 * q.size * length, 2 * q.size * 14, 2 * q.size * length // HEAD),
        name="back_and_sum",
    )(q, qm, g, lse, k, km, v, tokens, rem_tokens, *weights, vg, vu, *sources)


def finish_kernel(residual_ref, own_ref, rem_ref, *refs):
    ins, outs = refs[:7], refs[7:]
    total = residual_ref[...].astype(F32) + own_ref[...].astype(F32) + rem_ref[...].astype(F32)
    outs[0][...] = total.astype(BF16)

    @pl.when(pl.program_id(0) == 0)
    def _():
        for source, target in zip(ins[:6], outs[1:7]):
            target[...] = source[...]
        for i, target in enumerate(outs[7:]):
            target[...] = ins[6][i, : target.shape[0]]


def finish(residual, own, rem, matrices, vectors, shares):
    seqs, length, features = own.shape
    row_spec = pl.BlockSpec((1, length, features), lambda s: (s, 0, 0))

    def fixed(shape):
        return pl.BlockSpec(shape, lambda s: (0,) * len(shape))

    shapes = [m.shape for m in matrices] + [(n,) for n in shares]
    return pl.pallas_call(
        finish_kernel,
        grid=(seqs,),
        in_specs=[row_spec] * 3 + [fixed(m.shape) for m in matrices] + [fixed(vectors.shape)],
        out_specs=[row_spec] + [fixed(s) for s in shapes],
        out_shape=[jax.ShapeDtypeStruct(own.shape, BF16)] + [jax.ShapeDtypeStruct(s, F32) for s in shapes],
        compiler_params=params(60),
        cost_estimate=cost(2 * own.size, 8 * own.size),
        name="finish",
    )(residual, own, rem, *matrices, vectors)


def back_plainly(q, qm, o, g, lse, own, rem, bg, tokens, rem_tokens, weights, dwd, dwu, dwo, vg, vu):
    seqs, length, features = q.shape
    dp, blk = lax.axis_size("dp"), lax.axis_size("blk")
    dq, dko, dvo, dkr, dvr = attend_back(q, qm, o, g, lse, own, rem)
    rem_gradient = tokens_back(rem_back_kernel, (dkr, dvr), weights[1:])
    came = [
        lax.ppermute(part, "blk", [((i + r) % blk, i) for i in range(blk)])
        for r, part in enumerate(jnp.split(rem_gradient, blk - 1, axis=1), 1)
    ]
    flat = [v.reshape(-1, features) for v in (tokens, rem_tokens, dq, dko, dvo, dkr, dvr)]
    dwq, dwk, dwv, dbq, dbv = weights_back(*flat)
    total = tokens_back(own_back_kernel, (bg, dq, dko, dvo), weights).astype(F32)
    for part in came:
        total += part.astype(F32)
    dwu = jnp.moveaxis(dwu[0], 0, 1).reshape(features, -1)
    summed = [scatter_sum(w) for w in (dwd, dwu, dwo, dwq, dwk, dwv)]
    rows = [vg[i] for i in range(6)] + [dbq, dbv, vu]
    rows = [scatter_sum(v.reshape(dp * blk, -1)) for v in rows]
    return [total.astype(BF16)] + summed + [[v[0] for v in rows]]


def body(
    tokens,
    query_weight,
    query_bias,
    key_weight,
    value_weight,
    value_bias,
    out_weight,
    out_bias,
    gain_one,
    shift_one,
    up_weight,
    up_bias,
    down_weight,
    down_bias,
    gain_two,
    shift_two,
    group_ids,
    valid_mask,
    cotangent,
):
    seqs, length, features = tokens.shape
    rows = seqs * length
    blk = lax.axis_size("blk")

    def from_others(value):
        found = [
            lax.ppermute(value, "blk", [(i, (i + r) % blk) for i in range(blk)])
            for r in range(1, blk)
        ]
        return found[0] if len(found) == 1 else jnp.concatenate(found, axis=1)

    codes = jnp.where(valid_mask == 1, group_ids, -1)
    dp = lax.axis_size("dp")
    by_kernel = blk == 2 and dp & (dp - 1) == 0 and dp > 1 and (features // dp) % 16 == 0
    projections = (query_weight, key_weight, value_weight)
    vectors = (
        query_bias,
        value_bias,
        out_bias,
        gain_one,
        shift_one,
        down_bias,
        gain_two,
        shift_two,
    )

    if by_kernel:
        (block_out, branch_gradient, attended_gradient, attended, lse, query_mask, key_masks,
         first_t, feed_t, vector_gradients, up_bias_gradient, queries, keys, values,
         rem_tokens, active, inner_gradient) = front(
            tokens,
            group_ids,
            valid_mask,
            cotangent,
            vectors,
            up_bias,
            projections + (out_weight, up_weight, down_weight),
        )
        dwu, dwd, dwo = feed_weights(
            first_t,
            inner_gradient.reshape(rows, -1),
            feed_t,
            active.reshape(rows, -1),
            attended.reshape(rows, features),
            branch_gradient.reshape(rows, features),
        )
        own_gradient, rem_gradient, *matrices, vectors = back_and_sum(
            queries,
            query_mask,
            attended_gradient,
            lse,
            keys,
            key_masks,
            values,
            tokens,
            rem_tokens,
            projections,
            dwd,
            dwu,
            dwo,
            vector_gradients,
            up_bias_gradient,
        )
        shares = [features // (dp * blk)] * 8 + [up_bias.size // (dp * blk)]
        found = finish(branch_gradient, own_gradient, rem_gradient, matrices, vectors, shares)
        tokens_gradient, dwd, dwu, dwo, dwq, dwk, dwv, *rows_left = found
    else:
        rem_tokens = from_others(tokens)
        rem_codes = from_others(codes.astype(BF16)).astype(jnp.int32)
        slot = jnp.arange(PAIR, dtype=jnp.int32) % HEAD

        def key_mask(code):
            return jnp.where(code[:, :, None] == slot, 0.0, MASKED).astype(BF16)

        query_mask = (group_ids[:, :, None] == slot).astype(BF16)
        vectors = jnp.stack(vectors).astype(F32)
        queries, own_keys, own_values = project(tokens, vectors, projections)
        rem_keys, rem_values = project(rem_tokens, vectors, projections[1:])
        own = (own_keys, key_mask(codes), own_values)
        rem = (rem_keys, key_mask(rem_codes), rem_values)
        attended, lse = attend(queries, query_mask, own, rem)
        (block_out, branch_gradient, attended_gradient, vector_gradients, up_bias_gradient,
         dwu, dwd, dwo) = feed_both_ways(
            tokens.reshape(rows, features),
            attended.reshape(rows, features),
            cotangent.reshape(rows, features),
            vectors[2:],
            up_bias.astype(F32)[None],
            out_weight,
            up_weight,
            down_weight,
            1,
        )
        tokens_gradient, dwd, dwu, dwo, dwq, dwk, dwv, rows_left = back_plainly(
            queries,
            query_mask,
            attended,
            attended_gradient.reshape(tokens.shape),
            lse,
            own,
            rem,
            branch_gradient.reshape(tokens.shape),
            tokens,
            rem_tokens,
            projections,
            dwd,
            dwu,
            dwo,
            vector_gradients,
            up_bias_gradient,
        )
    dbo, dg1, ds1, dbd, dg2, ds2, dbq, dbv, dbu = rows_left
    return (
        block_out.reshape(tokens.shape),
        tokens_gradient,
        dwq,
        dbq,
        dwk,
        dwv,
        dbv,
        dwo,
        dbo,
        dg1,
        ds1,
        dwu,
        dbu,
        dwd,
        dbd,
        dg2,
        ds2,
    )


def solution(mesh):
    rows, shared, pair = P("dp", "blk", None), P(), P("dp", "blk")
    matrix, vector = P(("dp", "blk"), None), P(("dp", "blk"))
    return jax.shard_map(
        body,
        mesh=mesh,
        in_specs=(rows,) + (shared,) * 15 + (pair, pair, rows),
        out_specs=(
            rows,
            rows,
            matrix,
            vector,
            matrix,
            matrix,
            vector,
            matrix,
            vector,
            vector,
            vector,
            matrix,
            vector,
            matrix,
            vector,
            vector,
            vector,
        ),
        check_vma=False,
    )
```

profile of v0, /device:TPU:0, one launch (start us, length us, event | category | flops | bytes accessed | tf_op | source)
XLA Modules:
  0.0 284.8 jit_solution(13283044507209028683)
XLA Ops:
  0.7 118.8 %front.1 = (bf16[3,512,768]{2,1,0:T(8,128)(2,1)}, bf16[3,512,768]{2,1,0:T(8,128)(2,1)}, bf16[3,512,768]{2,1,0:T(8,128)(2,1)}, bf16[3,512,768]{2,1,0:T(8,128)(2,1...) custom-call(bf16[3,512,768]{2,1,0:T(8,128)(2,1)} %refs_7_.1, ...), custom_call_target="tpu_custom_call" | custom-call | flops 54962159616 | bytes 47185920 | tf_op jit(solution)/shard_map/front/pallas_call | solution.py:667
  119.5 26.7 %feed_weights.1 = (bf16[8,4,48,768]{3,2,1,0:T(8,128)(2,1)}, bf16[8,192,768]{2,1,0:T(8,128)(2,1)}, bf16[8,48,768]{2,1,0:T(8,128)(2,1)}) custom-call(bf16[768,1536]{1,0:T(8,128)(2,1)} %get-tuple-element.74.first_ref, bf16[1536,3072]{1,0:T(8,128)(2,1)} %bitcast.9, bf16[768,1536]{1,0:T(8,128)(2,1)} %get-tuple-element.76.feed_ref, bf16[1536,3072]{1,0:T(8,128)(2,1)} %bitcast.8, ...), custom_call_target="tpu_custom_call" | custom-call | flops 16307453952 | bytes 28311552 | tf_op jit(solution)/shard_map/feed_weights/pallas_call | solution.py:809
  146.1 130.9 %back_and_sum.1 = (bf16[3,512,768]{2,1,0:T(8,128)(2,1)}, bf16[3,512,768]{2,1,0:T(8,128)(2,1)}, f32[96,768]{1,0:T(8,128)}, f32[24,3072]{1,0:T(8,128)}, f32[24,768...) custom-call(bf16[3,512,768]{2,1,0:T(8,128)(2,1)} %get-tuple-element.64.refs_0_, ...), custom_call_target="tpu_custom_call" | custom-call | flops 48318382080 | bytes 33030144 | tf_op jit(solution)/shard_map/back_and_sum/pallas_call | solution.py:1404
  277.0 0.0 copy-start
  277.0 6.4 %finish.1 = (bf16[3,512,768]{2,1,0:T(8,128)(2,1)}, f32[96,768]{1,0:T(8,128)}, f32[24,3072]{1,0:T(8,128)}, f32[24,768]{1,0:T(8,128)}, f32[24,768]{1,0:T(8,128)}, ...) custom-call(bf16[3,512,768]{2,1,0:T(8,128)(2,1)} %get-tuple-element., ...), custom_call_target="tpu_custom_call" | custom-call | flops 2359296 | bytes 9437184 | tf_op jit(solution)/shard_map/finish/pallas_call | solution.py:1453
  283.4 0.0 copy-done
  283.4 1.4 copy.37
Async XLA Ops:
  277.0 6.4 %copy-start = (bf16[3,512,768]{2,1,0:T(8,128)(2,1)S(1)}, bf16[3,512,768]{2,1,0:T(8,128)(2,1)}, u32[]{:S(2)}) copy-start(bf16[3,512,768]{2,1,0:T(8,128)(2,1)} %get-tuple-element.124) | copy-start | bytes 7077892
where the time goes:
time: 285 us
  Pallas kernels  283 us (99%)
    pallas_call x1, Pallas kernels, back_and_sum(): pl.pallas_call(functools.partial(back_kernel, units, bits, groups, table,...  131 us
    pallas_call x1, Pallas kernels, front(): pl.pallas_call(front_kernel, grid=(seqs,), in_specs=[anywhere, whole_spec...  119 us
    pallas_call x1, Pallas kernels, feed_weights(): pl.pallas_call(functools.partial(feed_weights_kernel, blocks), grid=(bloc...  26.7 us
    pallas_call x1, Pallas kernels, finish(): pl.pallas_call(finish_kernel, grid=(seqs,), in_specs=[row_spec] * 3 + [fi...  6.4 us

commit v1 on v0

--- a/solution.py
+++ b/solution.py
@@ -978,7 +978,7 @@
         else:
             us = units[which].rows * units[which].columns * 2e-5
             us *= 1 << max(bits - 1 - step, 0)
-            us *= {0: 0.4, bits - 1: 3.0}.get(step, 1.2)
+            us *= {0: 0.4, bits - 1: 3.0}.get(step, 1.25)
             link = {0: "core", bits - 1: "far", bits: "blk"}.get(step, "near")
         start = max(now, free.get(link, 0.0))
         if link:
@@ -1349,7 +1349,7 @@
     for h in range(groups):
         columns = slice(h * width, (h + 1) * width)
         units.append(Unit(None, 3 * low, width, 3, [(3 + i, every, columns) for i in range(3)]))
-    table, tail = timetable(units, bits, seqs, groups, 4.2, length * features * 4e-5)
+    table, tail = timetable(units, bits, seqs, groups, 3.9, length * features * 4e-5)
 
     half = low // 2
     out_shape = [

time: 285 us -> 280 us (0.982)
  Pallas kernels: 283 us -> 278 us
    pallas_call x1, Pallas kernels: 131 us -> 126 us  [back_and_sum(): pl.pallas_call(functools.partial(back_kernel, units, bits, groups, table,...]
where the time goes in v1:
time: 280 us
  Pallas kernels  278 us (99%)
    pallas_call x1, Pallas kernels, back_and_sum(): pl.pallas_call(functools.partial(back_kernel, units, bits, groups, table,...  126 us
    pallas_call x1, Pallas kernels, front(): pl.pallas_call(front_kernel, grid=(seqs,), in_specs=[anywhere, whole_spec...  119 us
    pallas_call x1, Pallas kernels, feed_weights(): pl.pallas_call(functools.partial(feed_weights_kernel, blocks), grid=(bloc...  26.7 us
    pallas_call x1, Pallas kernels, finish(): pl.pallas_call(finish_kernel, grid=(seqs,), in_specs=[row_spec] * 3 + [fi...  6.4 us

profile of v1, /device:TPU:0, one launch (start us, length us, event | category | flops | bytes accessed | tf_op | source)
XLA Modules:
  0.0 279.8 jit_solution(13533648506821839052)
XLA Ops:
  0.7 118.8 %front.1 = (bf16[3,512,768]{2,1,0:T(8,128)(2,1)}, bf16[3,512,768]{2,1,0:T(8,128)(2,1)}, bf16[3,512,768]{2,1,0:T(8,128)(2,1)}, bf16[3,512,768]{2,1,0:T(8,128)(2,1...) custom-call(bf16[3,512,768]{2,1,0:T(8,128)(2,1)} %refs_7_.1, ...), custom_call_target="tpu_custom_call" | custom-call | flops 54962159616 | bytes 47185920 | tf_op jit(solution)/shard_map/front/pallas_call | solution.py:667
  119.5 26.7 %feed_weights.1 = (bf16[8,4,48,768]{3,2,1,0:T(8,128)(2,1)}, bf16[8,192,768]{2,1,0:T(8,128)(2,1)}, bf16[8,48,768]{2,1,0:T(8,128)(2,1)}) custom-call(bf16[768,1536]{1,0:T(8,128)(2,1)} %get-tuple-element.74.first_ref, bf16[1536,3072]{1,0:T(8,128)(2,1)} %bitcast.9, bf16[768,1536]{1,0:T(8,128)(2,1)} %get-tuple-element.76.feed_ref, bf16[1536,3072]{1,0:T(8,128)(2,1)} %bitcast.8, ...), custom_call_target="tpu_custom_call" | custom-call | flops 16307453952 | bytes 28311552 | tf_op jit(solution)/shard_map/feed_weights/pallas_call | solution.py:809
  146.1 125.9 %back_and_sum.1 = (bf16[3,512,768]{2,1,0:T(8,128)(2,1)}, bf16[3,512,768]{2,1,0:T(8,128)(2,1)}, f32[96,768]{1,0:T(8,128)}, f32[24,3072]{1,0:T(8,128)}, f32[24,768...) custom-call(bf16[3,512,768]{2,1,0:T(8,128)(2,1)} %get-tuple-element.64.refs_0_, ...), custom_call_target="tpu_custom_call" | custom-call | flops 48318382080 | bytes 33030144 | tf_op jit(solution)/shard_map/back_and_sum/pallas_call | solution.py:1404
  272.0 0.0 copy-start
  272.0 6.4 %finish.1 = (bf16[3,512,768]{2,1,0:T(8,128)(2,1)}, f32[96,768]{1,0:T(8,128)}, f32[24,3072]{1,0:T(8,128)}, f32[24,768]{1,0:T(8,128)}, f32[24,768]{1,0:T(8,128)}, ...) custom-call(bf16[3,512,768]{2,1,0:T(8,128)(2,1)} %get-tuple-element., ...), custom_call_target="tpu_custom_call" | custom-call | flops 2359296 | bytes 9437184 | tf_op jit(solution)/shard_map/finish/pallas_call | solution.py:1453
  278.4 0.0 copy-done
  278.4 1.4 copy.37
Async XLA Ops:
  272.0 6.4 %copy-start = (bf16[3,512,768]{2,1,0:T(8,128)(2,1)S(1)}, bf16[3,512,768]{2,1,0:T(8,128)(2,1)}, u32[]{:S(2)}) copy-start(bf16[3,512,768]{2,1,0:T(8,128)(2,1)} %get-tuple-element.124) | copy-start | bytes 7077892
